TPU v7x, 512 devices: a whole 4x8x8 slice. The times are simulated.
512 devices in a mesh: member: 16 (over x, z_lo), gx: 32 (over y, z_hi, core).
Axes of the slice: x: 4, y: 8, z: 8 (z_hi: 2, z_lo: 4; z = z_hi * 4 + z_lo), core: 2. Of those that a mesh axis runs over, the one named last changes fastest.
Arguments:
- background_fields: float32 [64, 16, 512, 128], P('member', None, 'gx'), may hold values from -6 to 6
- obs_col: int32 [2048], replicated, may hold values from 0 to 65535, as said below
- measured_height: int32 [2048], P('gx'), may hold values from 0 to 3
- obs_radius: int32 [2048], replicated, may hold values from 8 to 16
- obs_value: float32 [2048], P('gx'), may hold values from -8 to 8
- obs_var: float32 [2048], P('gx'), may hold values from 0.005 to 0.05
Outputs:
- analysis: float32 [64, 16, 512, 128], P('member', None, 'gx')
Inputs may be any that keep to these rules, and one draw needn't show every extreme that they name: `obs_col`: entries j * 64 to (j + 1) * 64 - 1 observe columns x * 128 + y with x from j * 16 to (j + 1) * 16 - 1.
All inputs are finite; a program needn't handle non-finite values.
Results may differ from a plain program's by a relative error of at most 0.0003.
Values sent between devices are 32-bit elements; how exact they have to be, the bound alone decides.
A program may use at most 64 MiB of HBM per device.

v0:
```python
import jax
import jax.numpy as jnp
from jax import lax
from jax.experimental import pallas as pl
from jax.experimental.pallas import tpu as pltpu
from jax.sharding import PartitionSpec as P

NS_ITERS = 6
COURANT = 0.6
DIFFUSE = 0.1
CHUNKS = 4
NS_PAIRS = 4
F32 = jnp.float32
BF16 = jnp.bfloat16
MESH = pl.DeviceIdType.MESH


def split2(x):
    hi = x.astype(BF16)
    lo = (x - hi.astype(F32)).astype(BF16)
    return hi, lo


def matmul(a, b):
    return lax.dot_general(a, b, (((1,), (0,)), ((), ())), preferred_element_type=F32)


def matmul_t(a, b):
    return lax.dot_general(a, b, (((1,), (1,)), ((), ())), preferred_element_type=F32)


def advance(west, center, east):
    shape = center.shape
    rows = center.reshape(-1, shape[-1])
    lane = lax.broadcasted_iota(jnp.int32, rows.shape, 1)
    south = jnp.where(lane == 0, 0.0, pltpu.roll(rows, 1, 1)).reshape(shape)
    north = jnp.where(lane == 127, 0.0, pltpu.roll(rows, 127, 1)).reshape(shape)
    return (
        center
        + COURANT * (west - center)
        + DIFFUSE * (west + east + south + north - 4.0 * center)
    )


def kernel(
    bg,
    col,
    radius,
    height,
    value,
    var,
    out,
    state,
    mid,
    fore,
    gathered,
    turned,
    weights,
    wgt,
    spread_ref,
    side,
    side_in,
    picked,
    stage,
    back,
    back_in,
    halo_send,
    halo_recv,
    side_send,
    side_recv,
    pick_send,
    pick_recv,
    fore_send,
    fore_recv,
    back_send,
    back_recv,
):
    me = lax.axis_index("member")
    tile = lax.axis_index("gx")
    group = 16
    tiles = lax.axis_size("gx")
    right = lax.rem(tile + 1, tiles)
    left = lax.rem(tile + tiles - 1, tiles)

    barrier = pltpu.get_barrier_semaphore()
    for other in (left, right):
        pl.semaphore_signal(barrier, inc=1, device_id={"gx": other}, device_id_type=MESH)

    def greet(d, carry):
        pl.semaphore_signal(
            barrier, inc=1, device_id={"member": lax.rem(me + d, group)}, device_id_type=MESH
        )
        return carry

    lax.fori_loop(1, group, greet, 0)

    def rearrange(x, carry):
        for k in range(4):
            rows = bg[pl.ds(k * 256 + x, 16, stride=16), :]
            for fh in range(4):
                state[x + 2, fh, 4 * k : 4 * k + 4, :] = rows[4 * fh : 4 * fh + 4]
        return carry

    lax.fori_loop(0, 16, rearrange, 0)
    pl.semaphore_wait(barrier, group - 1 + 2)

    def halo(direction, part):
        which = pl.ds(0, 1) if part == 0 else pl.ds(1, 3)
        src, dst, peer = ((16, 0, right), (2, 18, left))[direction]
        slot = direction * 2 + part
        return pltpu.make_async_remote_copy(
            src_ref=state.at[pl.ds(src, 2), which],
            dst_ref=state.at[pl.ds(dst, 2), which],
            send_sem=halo_send.at[slot],
            recv_sem=halo_recv.at[slot],
            device_id={"gx": peer},
            device_id_type=MESH,
        )

    for part in range(2):
        for direction in range(2):
            halo(direction, part).start()

    def first_step(index, which):
        mid[index, which] = advance(
            state[index, which], state[index + 1, which], state[index + 2, which]
        )

    def second_step(x, which):
        fore[x, which] = advance(mid[x, which], mid[x + 1, which], mid[x + 2, which])

    whole = pl.ds(0, 4)

    def inner_first(i, carry):
        first_step(i, whole)
        return carry

    def inner_second(i, carry):
        second_step(i, whole)
        return carry

    lax.fori_loop(2, 16, inner_first, 0)
    lax.fori_loop(2, 14, inner_second, 0)

    def outer_rows(part):
        which = pl.ds(0, 1) if part == 0 else pl.ds(1, 3)
        count = 1 if part == 0 else 3
        for direction in range(2):
            halo(direction, part).wait_recv()
        nothing = jnp.zeros((count, 16, 128), F32)

        @pl.when(tile == 0)
        def _():
            state[0, which] = nothing
            state[1, which] = nothing

        @pl.when(tile == tiles - 1)
        def _():
            state[18, which] = nothing
            state[19, which] = nothing

        for index in (0, 1, 16, 17):
            first_step(index, which)

        @pl.when(tile == 0)
        def _():
            mid[0, which] = nothing

        @pl.when(tile == tiles - 1)
        def _():
            mid[17, which] = nothing

        for x in (0, 1, 14, 15):
            second_step(x, which)

    outer_rows(0)

    def tile_row(ref, t):
        row = ref[pl.ds(t // 2, 1), :]
        return jnp.where(lax.rem(t, 2) == 0, row[:, :64], row[:, 64:])

    own_col = tile_row(col, tile)
    own_x = own_col // 128 - tile * 16
    own_y = lax.rem(own_col, 128)
    hot_y = (lax.broadcasted_iota(jnp.int32, (128, 64), 0) == own_y).astype(F32).astype(BF16)
    observed = fore[:, 0].reshape(256, 128)
    hi, lo = split2(observed)
    low = (observed - hi.astype(F32) - lo.astype(F32)).astype(BF16)
    along_y = (matmul(hi, hot_y) + matmul(lo, hot_y)) + matmul(low, hot_y)
    total = jnp.zeros((16, 64), F32)
    for x in range(16):
        total = total + jnp.where(own_x == x, along_y[16 * x : 16 * x + 16], 0.0)
    level = lax.rem(lax.broadcasted_iota(jnp.int32, (16, 64), 0), 4)
    total = jnp.where(level == height[...], total, 0.0)
    sampled = jnp.concatenate(
        [jnp.sum(total[4 * k : 4 * k + 4], axis=0, keepdims=True) for k in range(4)]
        + [value[...], var[...], jnp.zeros((2, 64), F32)],
        axis=0,
    )
    side[...] = jnp.concatenate([sampled, jnp.zeros((8, 64), F32)], axis=1)

    def to_side(direction):
        return pltpu.make_async_remote_copy(
            src_ref=side,
            dst_ref=side_in.at[direction],
            send_sem=side_send.at[direction],
            recv_sem=side_recv.at[direction],
            device_id={"gx": (right, left)[direction]},
            device_id_type=MESH,
        )

    for direction in range(2):
        to_side(direction).start()

    outer_rows(1)

    for direction in range(2):
        to_side(direction).wait_recv()
    from_left = side_in[0][:, :64]
    own = side[...][:, :64]
    from_right = side_in[1][:, :64]
    picked[me] = jnp.concatenate(
        [
            jnp.concatenate([from_left[:4], own[:4]], axis=1),
            jnp.concatenate([from_right[:4], jnp.zeros((4, 64), F32)], axis=1),
        ],
        axis=0,
    )

    def send_picked(d, peer, slot):
        return pltpu.make_async_remote_copy(
            src_ref=picked.at[slot],
            dst_ref=picked.at[slot],
            send_sem=pick_send.at[d],
            recv_sem=pick_recv.at[slot],
            device_id={"member": peer},
            device_id_type=MESH,
        )

    def send_fore(d, peer, slot):
        return pltpu.make_async_remote_copy(
            src_ref=fore.at[peer],
            dst_ref=gathered.at[:, pl.ds(pl.multiple_of(slot * 16, 16), 16), :],
            send_sem=fore_send.at[d],
            recv_sem=fore_recv.at[slot],
            device_id={"member": peer},
            device_id_type=MESH,
        )

    def over_peers(action):
        def body(d, carry):
            action(d, lax.rem(me + d, group))
            return carry

        lax.fori_loop(1, group, body, 0)

    over_peers(lambda d, peer: send_picked(d, peer, me).start())
    over_peers(lambda d, peer: send_fore(d, peer, me).start())
    gathered[:, pl.ds(pl.multiple_of(me * 16, 16), 16), :] = fore[me]

    def three(a, b, c, fill):
        return jnp.concatenate([a, b, c, jnp.full((1, 64), fill, a.dtype)], axis=1)

    before = jnp.maximum(tile - 1, 0)
    after = jnp.minimum(tile + 1, tiles - 1)
    near_col = three(tile_row(col, before), own_col, tile_row(col, after), 0)
    near_radius = three(
        tile_row(radius, before), tile_row(radius, tile), tile_row(radius, after), 1
    ).astype(F32)
    near_value = three(from_left[4:5], own[4:5], from_right[4:5], 0.0)
    near_var = three(from_left[5:6], own[5:6], from_right[5:6], 1.0)
    lane = lax.broadcasted_iota(jnp.int32, (1, 256), 1)
    first = jnp.where(tile == 0, 64, 0)
    last = jnp.where(tile == tiles - 1, 128, 192)
    valid = (lane >= first) & (lane < last)
    inverse = jnp.where(valid, 1.0 / near_var, 0.0)
    gap_along = (tile * 16 + me - near_col // 128).astype(F32)
    site = 4 * lax.broadcasted_iota(jnp.int32, (32, 256), 0)
    gap_across = (site - lax.rem(near_col, 128)).astype(F32)
    taper = jnp.maximum(
        0.0,
        1.0 - (gap_along * gap_along + gap_across * gap_across) / (near_radius * near_radius),
    )
    wgt[...] = taper * inverse

    over_peers(lambda d, peer: send_picked(d, peer, peer).wait_recv())
    ensemble = jnp.concatenate(
        [
            jnp.concatenate([picked[m][:4] for m in range(16)], axis=0),
            jnp.concatenate([picked[m][4:] for m in range(16)], axis=0),
        ],
        axis=1,
    )
    mean = jnp.sum(ensemble, axis=0, keepdims=True) / 64.0
    spread = ensemble - mean
    innovation = near_value - mean
    spread_ref[...] = spread
    spread_hi, spread_lo = split2(spread)
    across_obs = jnp.concatenate([spread_hi, spread_hi, spread_lo, spread_lo], axis=0)

    lane2 = lax.broadcasted_iota(jnp.int32, (64, 128), 1)
    row2 = lax.broadcasted_iota(jnp.int32, (64, 128), 0)
    is_first = lane2 < 64
    eye = (lax.rem(lane2, 64) == row2).astype(F32)
    is_first_row = lax.broadcasted_iota(jnp.int32, (1, 128), 1) < 64

    def operand(x):
        hi, lo = split2(x)
        return jnp.concatenate([hi, lo], axis=1)

    def stationary(x):
        hi = x.astype(BF16).astype(F32)
        lo = x - hi
        zero = jnp.zeros_like(x)
        top = jnp.concatenate(
            [jnp.where(is_first, hi, zero), jnp.where(is_first, lo, zero)], axis=1
        ).astype(BF16)
        bottom = jnp.concatenate(
            [jnp.where(is_first, zero, hi), jnp.where(is_first, zero, lo)], axis=1
        ).astype(BF16)
        return jnp.concatenate([top, bottom, top, bottom], axis=0)

    def fold(x):
        return x[:, :128] + x[:, 128:]

    def solve(batch, carry):
        pairs = [batch * NS_PAIRS + i for i in range(NS_PAIRS)]
        system, drive = [], []
        for p in pairs:
            scaled = [spread_ref[...] * wgt[pl.ds(2 * p + h, 1), :] for h in range(2)]
            both = jnp.concatenate(scaled, axis=0)
            hi, lo = split2(both)
            product = fold(matmul_t(hi, across_obs)) + matmul_t(lo, across_obs[:128])
            system.append(jnp.where(is_first, product[:64], product[64:]) + 63.0 * eye)
            sums = [jnp.sum(s * innovation, axis=1, keepdims=True) for s in scaled]
            drive.append(jnp.where(is_first, sums[0], sums[1]))
        inv_norm, power, root = [], [], []
        for s in system:
            squares = jnp.sum(s * s, axis=0, keepdims=True)
            one = jnp.sum(jnp.where(is_first_row, squares, 0.0), axis=1, keepdims=True)
            two = jnp.sum(jnp.where(is_first_row, 0.0, squares), axis=1, keepdims=True)
            inv = 1.0 / jnp.sqrt(jnp.where(is_first_row, one, two))
            inv_norm.append(inv)
            power.append(s * inv)
        root = [1.5 * eye - 0.5 * p for p in power]
        for sweep in range(NS_ITERS - 1):
            fixed = [stationary(p) for p in power]
            moving = [operand(p) for p in power]
            if sweep == 0:
                square = [fold(matmul(m, f)) for m, f in zip(moving, fixed)]
            else:
                stacked = [
                    fold(matmul(jnp.concatenate([m, operand(z)], axis=0), f))
                    for m, z, f in zip(moving, root, fixed)
                ]
                square = [s[:64] for s in stacked]
                root = [1.5 * z - 0.5 * s[64:] for z, s in zip(root, stacked)]
            cube = [fold(matmul(operand(s), f)) for s, f in zip(square, fixed)]
            power = [2.25 * p - 1.5 * s + 0.25 * c for p, s, c in zip(power, square, cube)]
        root = [
            1.5 * z - 0.5 * fold(matmul(operand(z), stationary(p))) for z, p in zip(root, power)
        ]
        for p, z, inv, d in zip(pairs, root, inv_norm, drive):
            through = jnp.sum(z * d, axis=0, keepdims=True)
            again = z * through
            one = jnp.sum(jnp.where(is_first, again, 0.0), axis=1, keepdims=True)
            two = jnp.sum(jnp.where(is_first, 0.0, again), axis=1, keepdims=True)
            w = jnp.sqrt(63.0 * inv) * z + jnp.where(is_first, one, two) * inv
            w = w + (1.0 - jnp.sum(w, axis=0, keepdims=True)) * (1.0 / 64.0)
            hi = w.astype(BF16).astype(F32)
            lo = w - hi
            weights[2 * p] = jnp.where(is_first, hi, pltpu.roll(lo, 64, 1)).astype(BF16)
            weights[2 * p + 1] = jnp.where(is_first, pltpu.roll(hi, 64, 1), lo).astype(BF16)
        return carry

    lax.fori_loop(0, 16 // NS_PAIRS, solve, 0)
    weights[32] = weights[31]
    weights[33] = jnp.zeros((64, 128), BF16)

    over_peers(lambda d, peer: send_fore(d, peer, peer).wait_recv())

    def turn(fh, carry):
        for fl in range(4):
            rows = gathered[fh, pl.ds(fl, 64, stride=4), :]
            turned[fh * 4 + fl] = jnp.concatenate([rows, rows], axis=0).T
        return carry

    lax.fori_loop(0, 4, turn, 0)

    y8 = lax.broadcasted_iota(jnp.int32, (1, 8, 128), 1).astype(F32) * 0.25
    half = lax.broadcasted_iota(jnp.int32, (1, 8, 128), 2) < 64
    tent = [jnp.maximum(0.0, 1.0 - jnp.abs(y8 - c)) for c in range(3)]
    coef_a = jnp.where(half, tent[0], tent[1])
    coef_b = jnp.where(half, tent[2], 0.0)

    def send_back(q, d, peer, slot):
        return pltpu.make_async_remote_copy(
            src_ref=back.at[q, pl.ds(pl.multiple_of(peer * 16, 16), 16), :],
            dst_ref=back_in.at[q, slot],
            send_sem=back_send.at[q, d],
            recv_sem=back_recv.at[q, slot],
            device_id={"member": peer},
            device_id_type=MESH,
        )

    def apply(step, carry):
        q = CHUNKS - 1 - step
        for part in range(4):
            block = q * 4 + part
            rows = turned[:, pl.ds(pl.multiple_of(block * 8, 8), 8), :]
            near = operand((rows * coef_a).reshape(128, 128))
            far = operand((rows * coef_b).reshape(128, 128))
            c01 = weights[pl.ds(2 * block, 2)].reshape(128, 128)
            c23 = weights[pl.ds(2 * block + 2, 2)].reshape(128, 128)
            product = matmul(near, jnp.concatenate([c01, c01], axis=0)) + matmul(
                far, jnp.concatenate([c23, c23], axis=0)
            )
            product = (product[:, :64] + product[:, 64:]).reshape(4, 4, 8, 64)
            for fl in range(4):
                stage[:, fl * 32 + part * 8 : fl * 32 + part * 8 + 8, :] = product[:, fl]
        for fh in range(4):
            back[q, pl.ds(fh, 64, stride=4), :] = stage[fh].T
        over_peers(lambda d, peer: send_back(q, d, peer, me).start())
        back_in[q, me] = back[q, pl.ds(pl.multiple_of(me * 16, 16), 16), :]
        return carry

    lax.fori_loop(0, CHUNKS, apply, 0)

    for part in range(2):
        for direction in range(2):
            halo(direction, part).wait_send()
    for direction in range(2):
        to_side(direction).wait_send()
    over_peers(lambda d, peer: send_picked(d, peer, me).wait_send())
    over_peers(lambda d, peer: send_fore(d, peer, me).wait_send())
    for q in range(CHUNKS - 1, -1, -1):
        over_peers(lambda d, peer, q=q: send_back(q, d, peer, me).wait_send())
        over_peers(lambda d, peer, q=q: send_back(q, d, peer, peer).wait_recv())

    lane16 = lax.broadcasted_iota(jnp.int32, (16, 128), 1)

    def place(x, carry):
        chunks = [back_in[q, x] for q in range(4)]
        for fl in range(4):
            moved = [
                chunks[q] if q == fl else pltpu.roll(chunks[q], ((q - fl) * 32) % 128, 1)
                for q in range(4)
            ]
            low_half = jnp.where(lane16 < 32, moved[0], moved[1])
            high_half = jnp.where(lane16 < 96, moved[2], moved[3])
            out[pl.ds(fl * 16 + x, 16, stride=64), :] = jnp.where(
                lane16 < 64, low_half, high_half
            )
        return carry

    lax.fori_loop(0, 16, place, 0)


def per_device(background_fields, obs_col, measured_height, obs_radius, obs_value, obs_var):
    dma = pltpu.SemaphoreType.DMA
    result = pl.pallas_call(
        kernel,
        out_shape=jax.ShapeDtypeStruct((1024, 128), F32),
        in_specs=[pl.BlockSpec(memory_space=pltpu.VMEM)] * 6,
        out_specs=pl.BlockSpec(memory_space=pltpu.VMEM),
        scratch_shapes=[
            pltpu.VMEM((20, 4, 16, 128), F32),
            pltpu.VMEM((18, 4, 16, 128), F32),
            pltpu.VMEM((16, 4, 16, 128), F32),
            pltpu.VMEM((4, 256, 128), F32),
            pltpu.VMEM((16, 128, 128), F32),
            pltpu.VMEM((34, 64, 128), BF16),
            pltpu.VMEM((32, 256), F32),
            pltpu.VMEM((64, 256), F32),
            pltpu.VMEM((8, 128), F32),
            pltpu.VMEM((2, 8, 128), F32),
            pltpu.VMEM((16, 8, 128), F32),
            pltpu.VMEM((4, 128, 64), F32),
            pltpu.VMEM((CHUNKS, 256, 128), F32),
            pltpu.VMEM((CHUNKS, 16, 16, 128), F32),
            dma((4,)),
            dma((4,)),
            dma((2,)),
            dma((2,)),
            dma((16,)),
            dma((16,)),
            dma((16,)),
            dma((16,)),
            dma((CHUNKS, 16)),
            dma((CHUNKS, 16)),
        ],
        compiler_params=pltpu.CompilerParams(
            collective_id=0, has_side_effects=True, vmem_limit_bytes=40 * 1024 * 1024
        ),
    )(
        background_fields.reshape(1024, 128),
        obs_col.reshape(16, 128),
        obs_radius.reshape(16, 128),
        measured_height.reshape(1, 64),
        obs_value.reshape(1, 64),
        obs_var.reshape(1, 64),
    )
    return result.reshape(4, 16, 16, 128)


def solution(mesh):
    return jax.shard_map(
        per_device,
        mesh=mesh,
        in_specs=(P("member", None, "gx", None), P(), P("gx"), P(), P("gx"), P("gx")),
        out_specs=P("member", None, "gx", None),
        check_vma=False,
    )
```

profile of v0, /device:TPU:24, one launch (start us, length us, event | category | flops | bytes accessed | tf_op | source)
XLA Modules:
  0.0 56.9 jit_solution(14807564648084178496)
XLA Ops:
  0.0 0.0 copy-start.1
  0.0 0.0 copy-start.3
  0.0 0.0 copy-start.4
  0.0 0.0 copy-start.5
  0.0 0.7 %copy-done.1 = s32[2048]{0:T(1024)S(1)} copy-done((s32[2048]{0:T(1024)S(1)}, s32[2048]{0:T(1024)}, u32[]{:S(2)}) %copy-start.1) | copy-done | bytes 8216
  0.7 0.0 copy-done.3
  0.7 0.0 copy-done.4
  0.7 0.0 copy-done.5
  0.7 0.0 copy-start
  0.7 1.0 %copy-done = f32[4,16,16,128]{3,2,1,0:T(8,128)S(1)} copy-done((f32[4,16,16,128]{3,2,1,0:T(8,128)S(1)}, f32[4,16,16,128]{3,2,1,0:T(8,128)}, u32[]{:S(2)}) %copy-start) | copy-done | bytes 524312
  1.7 0.0 copy-start.2
  1.8 0.7 %copy-done.2 = s32[2048]{0:T(1024)S(1)} copy-done((s32[2048]{0:T(1024)S(1)}, s32[2048]{0:T(1024)}, u32[]{:S(2)}) %copy-start.2) | copy-done | bytes 8216
  2.4 53.7 %shard_map.64 = f32[1024,128]{1,0:T(8,128)S(1)} custom-call(f32[1024,128]{1,0:T(8,128)S(1)} %bitcast.8, s32[16,128]{1,0:T(8,128)S(1)} %bitcast.9, s32[16,128]{1,0:T(8,128)S(1)} %bitcast.10, s32[1,64]{1,0:T(1,128)S(1)} %bitcast.11, f32[1,64]{1,0:T(1,128)S(1)} %bitcast.12, f32[1,64]{1,0:T(1,128)S(1)} %bitcast.13), custom_call_target="tpu_custom_call" | custom-call | tf_op jit(solution)/shard_map/pallas_call | solution.py:461
  56.1 0.8 %copy.8 = f32[4,16,16,128]{3,2,1,0:T(8,128)} copy(f32[4,16,16,128]{3,2,1,0:T(8,128)S(1)} %bitcast.7) | data formatting | bytes 1048576
Async XLA Ops:
  0.0 0.7 %copy-start.1 = (s32[2048]{0:T(1024)S(1)}, s32[2048]{0:T(1024)}, u32[]{:S(2)}) copy-start(s32[2048]{0:T(1024)} %param.7) | copy-start | bytes 24580
  0.0 0.7 %copy-start.3 = (s32[64]{0:T(128)S(1)}, s32[64]{0:T(128)}, u32[]{:S(2)}) copy-start(s32[64]{0:T(128)} %param.8) | copy-start | bytes 772
  0.0 0.7 %copy-start.4 = (f32[64]{0:T(128)S(1)}, f32[64]{0:T(128)}, u32[]{:S(2)}) copy-start(f32[64]{0:T(128)} %param.10) | copy-start | bytes 772
  0.0 0.7 %copy-start.5 = (f32[64]{0:T(128)S(1)}, f32[64]{0:T(128)}, u32[]{:S(2)}) copy-start(f32[64]{0:T(128)} %param.11) | copy-start | bytes 772
  0.7 1.0 %copy-start = (f32[4,16,16,128]{3,2,1,0:T(8,128)S(1)}, f32[4,16,16,128]{3,2,1,0:T(8,128)}, u32[]{:S(2)}) copy-start(f32[4,16,16,128]{3,2,1,0:T(8,128)} %param.6) | copy-start | bytes 1572868
  1.7 0.7 %copy-start.2 = (s32[2048]{0:T(1024)S(1)}, s32[2048]{0:T(1024)}, u32[]{:S(2)}) copy-start(s32[2048]{0:T(1024)} %param.9) | copy-start | bytes 24580
where the time goes:
time: 57.2 us; the launch traced here: 56.9 us
  Pallas kernels  53.7 us (94%)
  local copies, waits for them, and re-layouts  3.22 us (6%)
    pallas_call x1, Pallas kernels, per_device(): pl.pallas_call(kernel, out_shape=jax.ShapeDtypeStruct((1024, 128), F32),...  53.7 us
    unnamed x13, local copies, waits for them, and re-layouts  3.22 us

commit v1 on v0

--- a/solution.py
+++ b/solution.py
@@ -10,6 +10,7 @@
 DIFFUSE = 0.1
 CHUNKS = 4
 NS_PAIRS = 4
+EARLY = 6
 F32 = jnp.float32
 BF16 = jnp.bfloat16
 MESH = pl.DeviceIdType.MESH
@@ -43,13 +44,19 @@
 
 
 def kernel(
+    bg_hbm,
+    col_hbm,
+    radius_hbm,
+    height_hbm,
+    value_hbm,
+    var_hbm,
+    back_in,
     bg,
     col,
     radius,
     height,
     value,
     var,
-    out,
     state,
     mid,
     fore,
@@ -61,9 +68,10 @@
     side,
     side_in,
     picked,
+    picked_in,
     stage,
     back,
-    back_in,
+    load_sem,
     halo_send,
     halo_recv,
     side_send,
@@ -74,6 +82,7 @@
     fore_recv,
     back_send,
     back_recv,
+    keep_sem,
 ):
     me = lax.axis_index("member")
     tile = lax.axis_index("gx")
@@ -82,17 +91,43 @@
     right = lax.rem(tile + 1, tiles)
     left = lax.rem(tile + tiles - 1, tiles)
 
+    def load(i):
+        pairs = (
+            (bg_hbm, bg),
+            (value_hbm, value),
+            (var_hbm, var),
+            (col_hbm, col),
+            (height_hbm, height),
+            (radius_hbm, radius),
+        )
+        return pltpu.make_async_copy(*pairs[i], load_sem.at[i])
+
+    for i in range(6):
+        load(i).start()
+
     barrier = pltpu.get_barrier_semaphore()
-    for other in (left, right):
-        pl.semaphore_signal(barrier, inc=1, device_id={"gx": other}, device_id_type=MESH)
-
-    def greet(d, carry):
-        pl.semaphore_signal(
-            barrier, inc=1, device_id={"member": lax.rem(me + d, group)}, device_id_type=MESH
-        )
-        return carry
-
-    lax.fori_loop(1, group, greet, 0)
+
+    def over_three(action):
+        def body(d, carry):
+            peer = lax.rem(me + d, group)
+            action(0, d, {"member": peer, "gx": right})
+            action(2, d, {"member": peer, "gx": left})
+
+            @pl.when(d > 0)
+            def _():
+                action(1, d, {"member": peer})
+
+            return carry
+
+        lax.fori_loop(0, group, body, 0)
+
+    over_three(
+        lambda rel, d, device: pl.semaphore_signal(
+            barrier, inc=1, device_id=device, device_id_type=MESH
+        )
+    )
+    for i in range(6):
+        load(i).wait()
 
     def rearrange(x, carry):
         for k in range(4):
@@ -102,7 +137,14 @@
         return carry
 
     lax.fori_loop(0, 16, rearrange, 0)
-    pl.semaphore_wait(barrier, group - 1 + 2)
+    side[...] = jnp.concatenate(
+        [
+            jnp.concatenate([value[...], var[...]], axis=1),
+            jnp.zeros((7, 128), F32),
+        ],
+        axis=0,
+    )
+    pl.semaphore_wait(barrier, 3 * group - 1)
 
     def halo(direction, part):
         which = pl.ds(0, 1) if part == 0 else pl.ds(1, 3)
@@ -117,9 +159,22 @@
             device_id_type=MESH,
         )
 
-    for part in range(2):
-        for direction in range(2):
-            halo(direction, part).start()
+    def to_side(direction):
+        return pltpu.make_async_remote_copy(
+            src_ref=side,
+            dst_ref=side_in.at[direction],
+            send_sem=side_send.at[direction],
+            recv_sem=side_recv.at[direction],
+            device_id={"gx": (right, left)[direction]},
+            device_id_type=MESH,
+        )
+
+    for direction in range(2):
+        halo(direction, 0).start()
+    for direction in range(2):
+        to_side(direction).start()
+    for direction in range(2):
+        halo(direction, 1).start()
 
     def first_step(index, which):
         mid[index, which] = advance(
@@ -132,15 +187,48 @@
     whole = pl.ds(0, 4)
 
     def inner_first(i, carry):
-        first_step(i, whole)
+        for j in range(7):
+            first_step(2 + 7 * i + j, whole)
         return carry
 
     def inner_second(i, carry):
-        second_step(i, whole)
+        for j in range(6):
+            second_step(2 + 6 * i + j, whole)
         return carry
 
-    lax.fori_loop(2, 16, inner_first, 0)
-    lax.fori_loop(2, 14, inner_second, 0)
+    lax.fori_loop(0, 2, inner_first, 0)
+    lax.fori_loop(0, 2, inner_second, 0)
+
+    def send_fore(d, peer, slot):
+        return pltpu.make_async_remote_copy(
+            src_ref=fore.at[peer],
+            dst_ref=gathered.at[:, pl.ds(pl.multiple_of(slot * 16, 16), 16), :],
+            send_sem=fore_send.at[d],
+            recv_sem=fore_recv.at[slot],
+            device_id={"member": peer},
+            device_id_type=MESH,
+        )
+
+    def over_peers(action):
+        def body(d, carry):
+            action(d, lax.rem(me + d, group))
+            return carry
+
+        lax.fori_loop(1, group, body, 0)
+
+    def start_fore(turn):
+        def body(d, peer):
+            inner = (peer >= 2) & (peer < 14)
+            early = inner & (d <= EARLY)
+            now = (early, inner & (d > EARLY), jnp.logical_not(inner))[turn]
+
+            @pl.when(now)
+            def _():
+                send_fore(d, peer, me).start()
+
+        over_peers(body)
+
+    start_fore(0)
 
     def outer_rows(part):
         which = pl.ds(0, 1) if part == 0 else pl.ds(1, 3)
@@ -192,70 +280,31 @@
         total = total + jnp.where(own_x == x, along_y[16 * x : 16 * x + 16], 0.0)
     level = lax.rem(lax.broadcasted_iota(jnp.int32, (16, 64), 0), 4)
     total = jnp.where(level == height[...], total, 0.0)
-    sampled = jnp.concatenate(
-        [jnp.sum(total[4 * k : 4 * k + 4], axis=0, keepdims=True) for k in range(4)]
-        + [value[...], var[...], jnp.zeros((2, 64), F32)],
-        axis=0,
-    )
-    side[...] = jnp.concatenate([sampled, jnp.zeros((8, 64), F32)], axis=1)
-
-    def to_side(direction):
-        return pltpu.make_async_remote_copy(
-            src_ref=side,
-            dst_ref=side_in.at[direction],
-            send_sem=side_send.at[direction],
-            recv_sem=side_recv.at[direction],
-            device_id={"gx": (right, left)[direction]},
-            device_id_type=MESH,
-        )
-
-    for direction in range(2):
-        to_side(direction).start()
-
-    outer_rows(1)
-
-    for direction in range(2):
-        to_side(direction).wait_recv()
-    from_left = side_in[0][:, :64]
-    own = side[...][:, :64]
-    from_right = side_in[1][:, :64]
-    picked[me] = jnp.concatenate(
+    sums = [jnp.sum(total[4 * k : 4 * k + 4], axis=0, keepdims=True) for k in range(4)]
+    picked[...] = jnp.concatenate(
         [
-            jnp.concatenate([from_left[:4], own[:4]], axis=1),
-            jnp.concatenate([from_right[:4], jnp.zeros((4, 64), F32)], axis=1),
+            jnp.concatenate([sums[0], sums[1]], axis=1),
+            jnp.concatenate([sums[2], sums[3]], axis=1),
         ],
         axis=0,
     )
 
-    def send_picked(d, peer, slot):
+    def send_picked(rel, d, device):
         return pltpu.make_async_remote_copy(
-            src_ref=picked.at[slot],
-            dst_ref=picked.at[slot],
-            send_sem=pick_send.at[d],
-            recv_sem=pick_recv.at[slot],
-            device_id={"member": peer},
+            src_ref=picked,
+            dst_ref=picked_in.at[rel, me],
+            send_sem=pick_send.at[rel, d],
+            recv_sem=pick_recv.at[rel],
+            device_id=device,
             device_id_type=MESH,
         )
 
-    def send_fore(d, peer, slot):
-        return pltpu.make_async_remote_copy(
-            src_ref=fore.at[peer],
-            dst_ref=gathered.at[:, pl.ds(pl.multiple_of(slot * 16, 16), 16), :],
-            send_sem=fore_send.at[d],
-            recv_sem=fore_recv.at[slot],
-            device_id={"member": peer},
-            device_id_type=MESH,
-        )
-
-    def over_peers(action):
-        def body(d, carry):
-            action(d, lax.rem(me + d, group))
-            return carry
-
-        lax.fori_loop(1, group, body, 0)
-
-    over_peers(lambda d, peer: send_picked(d, peer, me).start())
-    over_peers(lambda d, peer: send_fore(d, peer, me).start())
+    over_three(lambda rel, d, device: send_picked(rel, d, device).start())
+    picked_in[1, me] = picked[...]
+    start_fore(1)
+
+    outer_rows(1)
+    start_fore(2)
     gathered[:, pl.ds(pl.multiple_of(me * 16, 16), 16), :] = fore[me]
 
     def three(a, b, c, fill):
@@ -267,8 +316,11 @@
     near_radius = three(
         tile_row(radius, before), tile_row(radius, tile), tile_row(radius, after), 1
     ).astype(F32)
-    near_value = three(from_left[4:5], own[4:5], from_right[4:5], 0.0)
-    near_var = three(from_left[5:6], own[5:6], from_right[5:6], 1.0)
+    for direction in range(2):
+        to_side(direction).wait_recv()
+    from_left, own, from_right = side_in[0, 0:1, :], side[0:1, :], side_in[1, 0:1, :]
+    near_value = three(from_left[:, :64], own[:, :64], from_right[:, :64], 0.0)
+    near_var = three(from_left[:, 64:], own[:, 64:], from_right[:, 64:], 1.0)
     lane = lax.broadcasted_iota(jnp.int32, (1, 256), 1)
     first = jnp.where(tile == 0, 64, 0)
     last = jnp.where(tile == tiles - 1, 128, 192)
@@ -283,13 +335,22 @@
     )
     wgt[...] = taper * inverse
 
-    over_peers(lambda d, peer: send_picked(d, peer, peer).wait_recv())
+    def arrived(rel):
+        count = 15 if rel == 1 else 16
+        pltpu.make_async_copy(
+            picked_in.at[rel, pl.ds(0, count)],
+            picked_in.at[rel, pl.ds(0, count)],
+            pick_recv.at[rel],
+        ).wait()
+
+    def by_member(rel):
+        rows = jnp.concatenate([picked_in[rel, m] for m in range(16)], axis=0)
+        return jnp.concatenate([rows[:, :64], rows[:, 64:]], axis=0)
+
+    for rel in range(3):
+        arrived(rel)
     ensemble = jnp.concatenate(
-        [
-            jnp.concatenate([picked[m][:4] for m in range(16)], axis=0),
-            jnp.concatenate([picked[m][4:] for m in range(16)], axis=0),
-        ],
-        axis=1,
+        [by_member(rel) for rel in range(3)] + [jnp.zeros((64, 64), F32)], axis=1
     )
     mean = jnp.sum(ensemble, axis=0, keepdims=True) / 64.0
     spread = ensemble - mean
@@ -323,7 +384,7 @@
     def fold(x):
         return x[:, :128] + x[:, 128:]
 
-    def solve(batch, carry):
+    def solve(batch):
         pairs = [batch * NS_PAIRS + i for i in range(NS_PAIRS)]
         system, drive = [], []
         for p in pairs:
@@ -371,21 +432,16 @@
             lo = w - hi
             weights[2 * p] = jnp.where(is_first, hi, pltpu.roll(lo, 64, 1)).astype(BF16)
             weights[2 * p + 1] = jnp.where(is_first, pltpu.roll(hi, 64, 1), lo).astype(BF16)
-        return carry
-
-    lax.fori_loop(0, 16 // NS_PAIRS, solve, 0)
-    weights[32] = weights[31]
-    weights[33] = jnp.zeros((64, 128), BF16)
-
-    over_peers(lambda d, peer: send_fore(d, peer, peer).wait_recv())
+
 
     def turn(fh, carry):
         for fl in range(4):
-            rows = gathered[fh, pl.ds(fl, 64, stride=4), :]
+            rows = jnp.concatenate(
+                [gathered[fh, pl.ds(fl + 4 * odd, 32, stride=8), :] for odd in range(2)], axis=0
+            )
             turned[fh * 4 + fl] = jnp.concatenate([rows, rows], axis=0).T
         return carry
 
-    lax.fori_loop(0, 4, turn, 0)
 
     y8 = lax.broadcasted_iota(jnp.int32, (1, 8, 128), 1).astype(F32) * 0.25
     half = lax.broadcasted_iota(jnp.int32, (1, 8, 128), 2) < 64
@@ -403,8 +459,24 @@
             device_id_type=MESH,
         )
 
-    def apply(step, carry):
+    def keep(q):
+        return pltpu.make_async_copy(
+            back.at[q, pl.ds(pl.multiple_of(me * 16, 16), 16), :],
+            back_in.at[q, me],
+            keep_sem.at[q],
+        )
+
+    def chunk(step, carry):
         q = CHUNKS - 1 - step
+        solve(q)
+
+        @pl.when(step == 0)
+        def _():
+            weights[32] = weights[31]
+            weights[33] = jnp.zeros((64, 128), BF16)
+            over_peers(lambda d, peer: send_fore(d, peer, peer).wait_recv())
+            lax.fori_loop(0, 4, turn, 0)
+
         for part in range(4):
             block = q * 4 + part
             rows = turned[:, pl.ds(pl.multiple_of(block * 8, 8), 8), :]
@@ -419,51 +491,77 @@
             for fl in range(4):
                 stage[:, fl * 32 + part * 8 : fl * 32 + part * 8 + 8, :] = product[:, fl]
         for fh in range(4):
-            back[q, pl.ds(fh, 64, stride=4), :] = stage[fh].T
+            rows = stage[fh].T
+            for odd in range(2):
+                back[q, pl.ds(fh + 4 * odd, 32, stride=8), :] = rows[32 * odd : 32 * odd + 32]
         over_peers(lambda d, peer: send_back(q, d, peer, me).start())
-        back_in[q, me] = back[q, pl.ds(pl.multiple_of(me * 16, 16), 16), :]
+        keep(q).start()
         return carry
 
-    lax.fori_loop(0, CHUNKS, apply, 0)
+    lax.fori_loop(0, CHUNKS, chunk, 0)
 
     for part in range(2):
         for direction in range(2):
             halo(direction, part).wait_send()
     for direction in range(2):
         to_side(direction).wait_send()
-    over_peers(lambda d, peer: send_picked(d, peer, me).wait_send())
+    over_three(lambda rel, d, device: send_picked(rel, d, device).wait_send())
     over_peers(lambda d, peer: send_fore(d, peer, me).wait_send())
     for q in range(CHUNKS - 1, -1, -1):
         over_peers(lambda d, peer, q=q: send_back(q, d, peer, me).wait_send())
         over_peers(lambda d, peer, q=q: send_back(q, d, peer, peer).wait_recv())
-
-    lane16 = lax.broadcasted_iota(jnp.int32, (16, 128), 1)
-
-    def place(x, carry):
-        chunks = [back_in[q, x] for q in range(4)]
-        for fl in range(4):
-            moved = [
-                chunks[q] if q == fl else pltpu.roll(chunks[q], ((q - fl) * 32) % 128, 1)
-                for q in range(4)
-            ]
-            low_half = jnp.where(lane16 < 32, moved[0], moved[1])
-            high_half = jnp.where(lane16 < 96, moved[2], moved[3])
-            out[pl.ds(fl * 16 + x, 16, stride=64), :] = jnp.where(
-                lane16 < 64, low_half, high_half
-            )
-        return carry
-
-    lax.fori_loop(0, 16, place, 0)
+        keep(q).wait()
+
+
+def place(back_in, out, landed, placed, load_sem, leave_sem):
+    lane = lax.broadcasted_iota(jnp.int32, (16, 128), 1)
+    flat = placed.reshape(2, 512, 128)
+
+    def load(part):
+        rows = pl.ds(4 * part, 4)
+        return pltpu.make_async_copy(back_in.at[:, rows], landed.at[:, rows], load_sem.at[part])
+
+    def leave(half):
+        return pltpu.make_async_copy(
+            placed.at[half], out.at[:, :, pl.ds(8 * half, 8), :], leave_sem.at[half]
+        )
+
+    for part in range(4):
+        load(part).start()
+    for half in range(2):
+        for x in range(8):
+            if x % 4 == 0:
+                load(2 * half + x // 4).wait()
+            chunks = [landed[q, 8 * half + x] for q in range(4)]
+            for fl in range(4):
+                moved = [
+                    chunks[q] if q == fl else pltpu.roll(chunks[q], ((q - fl) * 32) % 128, 1)
+                    for q in range(4)
+                ]
+                low_half = jnp.where(lane < 32, moved[0], moved[1])
+                high_half = jnp.where(lane < 96, moved[2], moved[3])
+                flat[half, pl.ds(fl * 8 + x, 16, stride=32), :] = jnp.where(
+                    lane < 64, low_half, high_half
+                )
+        leave(half).start()
+    for half in range(2):
+        leave(half).wait()
 
 
 def per_device(background_fields, obs_col, measured_height, obs_radius, obs_value, obs_var):
     dma = pltpu.SemaphoreType.DMA
     result = pl.pallas_call(
         kernel,
-        out_shape=jax.ShapeDtypeStruct((1024, 128), F32),
-        in_specs=[pl.BlockSpec(memory_space=pltpu.VMEM)] * 6,
-        out_specs=pl.BlockSpec(memory_space=pltpu.VMEM),
+        out_shape=jax.ShapeDtypeStruct((CHUNKS, 16, 16, 128), F32),
+        in_specs=[pl.BlockSpec(memory_space=pltpu.HBM)] * 6,
+        out_specs=pl.BlockSpec(memory_space=pltpu.HBM),
         scratch_shapes=[
+            pltpu.VMEM((1024, 128), F32),
+            pltpu.VMEM((16, 128), jnp.int32),
+            pltpu.VMEM((16, 128), jnp.int32),
+            pltpu.VMEM((1, 64), jnp.int32),
+            pltpu.VMEM((1, 64), F32),
+            pltpu.VMEM((1, 64), F32),
             pltpu.VMEM((20, 4, 16, 128), F32),
             pltpu.VMEM((18, 4, 16, 128), F32),
             pltpu.VMEM((16, 4, 16, 128), F32),
@@ -474,33 +572,52 @@
             pltpu.VMEM((64, 256), F32),
             pltpu.VMEM((8, 128), F32),
             pltpu.VMEM((2, 8, 128), F32),
-            pltpu.VMEM((16, 8, 128), F32),
+            pltpu.VMEM((2, 128), F32),
+            pltpu.VMEM((3, 16, 2, 128), F32),
             pltpu.VMEM((4, 128, 64), F32),
             pltpu.VMEM((CHUNKS, 256, 128), F32),
-            pltpu.VMEM((CHUNKS, 16, 16, 128), F32),
+            dma((6,)),
             dma((4,)),
             dma((4,)),
             dma((2,)),
             dma((2,)),
-            dma((16,)),
-            dma((16,)),
+            dma((3, 16)),
+            dma((3,)),
             dma((16,)),
             dma((16,)),
             dma((CHUNKS, 16)),
             dma((CHUNKS, 16)),
+            dma((CHUNKS,)),
         ],
         compiler_params=pltpu.CompilerParams(
-            collective_id=0, has_side_effects=True, vmem_limit_bytes=40 * 1024 * 1024
+            collective_id=0, has_side_effects=True, vmem_limit_bytes=64 * 1024 * 1024
         ),
     )(
-        background_fields.reshape(1024, 128),
-        obs_col.reshape(16, 128),
-        obs_radius.reshape(16, 128),
-        measured_height.reshape(1, 64),
-        obs_value.reshape(1, 64),
-        obs_var.reshape(1, 64),
-    )
-    return result.reshape(4, 16, 16, 128)
+        *(
+            pltpu.with_memory_space_constraint(x, pltpu.HBM)
+            for x in (
+                background_fields.reshape(1024, 128),
+                obs_col.reshape(16, 128),
+                obs_radius.reshape(16, 128),
+                measured_height.reshape(1, 64),
+                obs_value.reshape(1, 64),
+                obs_var.reshape(1, 64),
+            )
+        )
+    )
+    return pl.pallas_call(
+        place,
+        out_shape=jax.ShapeDtypeStruct((4, 16, 16, 128), F32),
+        in_specs=[pl.BlockSpec(memory_space=pltpu.HBM)],
+        out_specs=pl.BlockSpec(memory_space=pltpu.HBM),
+        scratch_shapes=[
+            pltpu.VMEM((CHUNKS, 16, 16, 128), F32),
+            pltpu.VMEM((2, 4, 16, 8, 128), F32),
+            dma((4,)),
+            dma((2,)),
+        ],
+        compiler_params=pltpu.CompilerParams(vmem_limit_bytes=60 * 1024 * 1024),
+    )(result)
 
 
 def solution(mesh):

time: 57.2 us -> 51.8 us (0.906)
  the two profiles are of different devices: /device:TPU:24 before, /device:TPU:1 now
where the time goes in v1:
time: 51.8 us; the launch traced here: 51.7 us
  Pallas kernels  51.7 us (100%)
    pallas_call x1, Pallas kernels, per_device(): pl.pallas_call(kernel, out_shape=jax.ShapeDtypeStruct((CHUNKS, 16, 16, 12...  49.2 us
    pallas_call x1, Pallas kernels, per_device(): pl.pallas_call(place, out_shape=jax.ShapeDtypeStruct((4, 16, 16, 128), F3...  2.46 us

profile of v1, /device:TPU:1, one launch (start us, length us, event | category | flops | bytes accessed | tf_op | source)
XLA Modules:
  0.0 51.7 jit_solution(15330534526625881961)
XLA Ops:
  0.0 49.2 %shard_map.64.back_in = f32[4,16,16,128]{3,2,1,0:T(8,128)} custom-call(f32[1024,128]{1,0:T(8,128)} %bitcast.6, s32[16,128]{1,0:T(8,128)} %bitcast.7, s32[16,128]{1,0:T(8,128)} %bitcast.8, s32[1,64]{1,0:T(1,128)} %bitcast.9, f32[1,64]{1,0:T(1,128)} %bitcast.10, f32[1,64]{1,0:T(1,128)} %bitcast.11), custom_call_target="tpu_custom_call" | custom-call | tf_op jit(solution)/shard_map/pallas_call | solution.py:553
  49.2 2.5 %shard_map.65 = f32[4,16,16,128]{3,2,1,0:T(8,128)} custom-call(f32[4,16,16,128]{3,2,1,0:T(8,128)} %shard_map.64.back_in), custom_call_target="tpu_custom_call" | custom-call | tf_op jit(solution)/shard_map/pallas_call | solution.py:608

commit v2 on v1

--- a/solution.py
+++ b/solution.py
@@ -8,9 +8,8 @@
 NS_ITERS = 6
 COURANT = 0.6
 DIFFUSE = 0.1
-CHUNKS = 4
-NS_PAIRS = 4
-EARLY = 6
+NS_PAIRS = 8
+EARLY = 1
 F32 = jnp.float32
 BF16 = jnp.bfloat16
 MESH = pl.DeviceIdType.MESH
@@ -199,36 +198,37 @@
     lax.fori_loop(0, 2, inner_first, 0)
     lax.fori_loop(0, 2, inner_second, 0)
 
-    def send_fore(d, peer, slot):
+    def send_fore(fh, peer):
         return pltpu.make_async_remote_copy(
-            src_ref=fore.at[peer],
-            dst_ref=gathered.at[:, pl.ds(pl.multiple_of(slot * 16, 16), 16), :],
-            send_sem=fore_send.at[d],
-            recv_sem=fore_recv.at[slot],
+            src_ref=fore.at[peer, fh],
+            dst_ref=gathered.at[fh, pl.ds(pl.multiple_of(me * 16, 16), 16), :],
+            send_sem=fore_send.at[fh],
+            recv_sem=fore_recv.at[fh],
             device_id={"member": peer},
             device_id_type=MESH,
         )
 
     def over_peers(action):
         def body(d, carry):
-            action(d, lax.rem(me + d, group))
+            action(lax.rem(me + d, group))
             return carry
 
         lax.fori_loop(1, group, body, 0)
 
-    def start_fore(turn):
-        def body(d, peer):
-            inner = (peer >= 2) & (peer < 14)
-            early = inner & (d <= EARLY)
-            now = (early, inner & (d > EARLY), jnp.logical_not(inner))[turn]
-
-            @pl.when(now)
+    def start_fore(groups, inner):
+        def body(peer):
+            is_inner = (peer >= 2) & (peer < 14)
+
+            @pl.when(is_inner if inner else jnp.logical_not(is_inner))
             def _():
-                send_fore(d, peer, me).start()
+                for fh in groups:
+                    send_fore(fh, peer).start()
 
         over_peers(body)
 
-    start_fore(0)
+    early, late = range(EARLY), range(EARLY, 4)
+    if EARLY:
+        start_fore(early, True)
 
     def outer_rows(part):
         which = pl.ds(0, 1) if part == 0 else pl.ds(1, 3)
@@ -301,10 +301,12 @@
 
     over_three(lambda rel, d, device: send_picked(rel, d, device).start())
     picked_in[1, me] = picked[...]
-    start_fore(1)
+    if EARLY:
+        start_fore(range(1), False)
+    start_fore(late, True)
 
     outer_rows(1)
-    start_fore(2)
+    start_fore(range(min(EARLY, 1), 4), False)
     gathered[:, pl.ds(pl.multiple_of(me * 16, 16), 16), :] = fore[me]
 
     def three(a, b, c, fill):
@@ -433,72 +435,78 @@
             weights[2 * p] = jnp.where(is_first, hi, pltpu.roll(lo, 64, 1)).astype(BF16)
             weights[2 * p + 1] = jnp.where(is_first, pltpu.roll(hi, 64, 1), lo).astype(BF16)
 
-
-    def turn(fh, carry):
+    y8 = lax.broadcasted_iota(jnp.int32, (1, 8, 128), 1).astype(F32) * 0.25
+    half = lax.broadcasted_iota(jnp.int32, (1, 8, 128), 2) < 64
+    tent = [jnp.maximum(0.0, 1.0 - jnp.abs(y8 - c)) for c in range(3)]
+    coef_a = jnp.where(half, tent[0], tent[1])
+    coef_b = jnp.where(half, tent[2], 0.0)
+
+    def all_bytes(buffer, sem):
+        rows = buffer.at[pl.ds(0, buffer.shape[0] // group * (group - 1))]
+        return pltpu.make_async_copy(rows, rows, sem)
+
+    def send_back(half, peer):
+        return pltpu.make_async_remote_copy(
+            src_ref=back.at[half, pl.ds(pl.multiple_of(peer * 32, 32), 32), :],
+            dst_ref=back_in.at[half, pl.ds(pl.multiple_of(me * 32, 32), 32), :],
+            send_sem=back_send.at[half],
+            recv_sem=back_recv.at[half],
+            device_id={"member": peer},
+            device_id_type=MESH,
+        )
+
+    def keep(half):
+        rows = pl.ds(pl.multiple_of(me * 32, 32), 32)
+        return pltpu.make_async_copy(
+            back.at[half, rows], back_in.at[half, rows], keep_sem.at[half]
+        )
+
+    def turn(fh):
         for fl in range(4):
             rows = jnp.concatenate(
                 [gathered[fh, pl.ds(fl + 4 * odd, 32, stride=8), :] for odd in range(2)], axis=0
             )
             turned[fh * 4 + fl] = jnp.concatenate([rows, rows], axis=0).T
-        return carry
-
-
-    y8 = lax.broadcasted_iota(jnp.int32, (1, 8, 128), 1).astype(F32) * 0.25
-    half = lax.broadcasted_iota(jnp.int32, (1, 8, 128), 2) < 64
-    tent = [jnp.maximum(0.0, 1.0 - jnp.abs(y8 - c)) for c in range(3)]
-    coef_a = jnp.where(half, tent[0], tent[1])
-    coef_b = jnp.where(half, tent[2], 0.0)
-
-    def send_back(q, d, peer, slot):
-        return pltpu.make_async_remote_copy(
-            src_ref=back.at[q, pl.ds(pl.multiple_of(peer * 16, 16), 16), :],
-            dst_ref=back_in.at[q, slot],
-            send_sem=back_send.at[q, d],
-            recv_sem=back_recv.at[q, slot],
-            device_id={"member": peer},
-            device_id_type=MESH,
-        )
-
-    def keep(q):
-        return pltpu.make_async_copy(
-            back.at[q, pl.ds(pl.multiple_of(me * 16, 16), 16), :],
-            back_in.at[q, me],
-            keep_sem.at[q],
-        )
-
-    def chunk(step, carry):
-        q = CHUNKS - 1 - step
-        solve(q)
+
+    def blend(half, part):
+        block = half * 8 + part
+        rows = turned[:, pl.ds(pl.multiple_of(block * 8, 8), 8), :]
+        near = operand((rows * coef_a).reshape(128, 128))
+        far = operand((rows * coef_b).reshape(128, 128))
+        c01 = weights[pl.ds(2 * block, 2)].reshape(128, 128)
+        c23 = weights[pl.ds(2 * block + 2, 2)].reshape(128, 128)
+        product = matmul(near, jnp.concatenate([c01, c01], axis=0)) + matmul(
+            far, jnp.concatenate([c23, c23], axis=0)
+        )
+        product = (product[:, :64] + product[:, 64:]).reshape(8, 2, 8, 64)
+        for odd in range(2):
+            stage[:, 64 * odd + 8 * part : 64 * odd + 8 * part + 8, :] = product[:, odd]
+
+    def half_step(step, carry):
+        half = 1 - step
+        solve(half)
 
         @pl.when(step == 0)
         def _():
             weights[32] = weights[31]
             weights[33] = jnp.zeros((64, 128), BF16)
-            over_peers(lambda d, peer: send_fore(d, peer, peer).wait_recv())
-            lax.fori_loop(0, 4, turn, 0)
-
-        for part in range(4):
-            block = q * 4 + part
-            rows = turned[:, pl.ds(pl.multiple_of(block * 8, 8), 8), :]
-            near = operand((rows * coef_a).reshape(128, 128))
-            far = operand((rows * coef_b).reshape(128, 128))
-            c01 = weights[pl.ds(2 * block, 2)].reshape(128, 128)
-            c23 = weights[pl.ds(2 * block + 2, 2)].reshape(128, 128)
-            product = matmul(near, jnp.concatenate([c01, c01], axis=0)) + matmul(
-                far, jnp.concatenate([c23, c23], axis=0)
-            )
-            product = (product[:, :64] + product[:, 64:]).reshape(4, 4, 8, 64)
-            for fl in range(4):
-                stage[:, fl * 32 + part * 8 : fl * 32 + part * 8 + 8, :] = product[:, fl]
-        for fh in range(4):
-            rows = stage[fh].T
+            for fh in range(4):
+                all_bytes(gathered.at[fh], fore_recv.at[fh]).wait()
+                turn(fh)
+
+        for part in range(8):
+            blend(half, part)
+        for pair in range(8):
+            rows = stage[pair].T
             for odd in range(2):
-                back[q, pl.ds(fh + 4 * odd, 32, stride=8), :] = rows[32 * odd : 32 * odd + 32]
-        over_peers(lambda d, peer: send_back(q, d, peer, me).start())
-        keep(q).start()
+                back[half, pl.ds(pair + 8 * odd, 32, stride=16), :] = rows[
+                    32 * odd : 32 * odd + 32
+                ]
+        over_peers(lambda peer: send_back(half, peer).start())
+        keep(half).start()
         return carry
 
-    lax.fori_loop(0, CHUNKS, chunk, 0)
+    lax.fori_loop(0, 2, half_step, 0)
 
     for part in range(2):
         for direction in range(2):
@@ -506,53 +514,45 @@
     for direction in range(2):
         to_side(direction).wait_send()
     over_three(lambda rel, d, device: send_picked(rel, d, device).wait_send())
-    over_peers(lambda d, peer: send_fore(d, peer, me).wait_send())
-    for q in range(CHUNKS - 1, -1, -1):
-        over_peers(lambda d, peer, q=q: send_back(q, d, peer, me).wait_send())
-        over_peers(lambda d, peer, q=q: send_back(q, d, peer, peer).wait_recv())
-        keep(q).wait()
+    for fh in range(4):
+        all_bytes(gathered.at[fh], fore_send.at[fh]).wait()
+    for half in range(2):
+        all_bytes(back.at[half], back_send.at[half]).wait()
+        keep(half).wait()
+    for half in range(2):
+        all_bytes(back.at[half], back_recv.at[half]).wait()
 
 
 def place(back_in, out, landed, placed, load_sem, leave_sem):
     lane = lax.broadcasted_iota(jnp.int32, (16, 128), 1)
-    flat = placed.reshape(2, 512, 128)
-
-    def load(part):
-        rows = pl.ds(4 * part, 4)
-        return pltpu.make_async_copy(back_in.at[:, rows], landed.at[:, rows], load_sem.at[part])
-
-    def leave(half):
-        return pltpu.make_async_copy(
-            placed.at[half], out.at[:, :, pl.ds(8 * half, 8), :], leave_sem.at[half]
-        )
-
-    for part in range(4):
-        load(part).start()
+
+    def load(half):
+        return pltpu.make_async_copy(back_in.at[half], landed.at[half], load_sem.at[half])
+
+    def leave(k):
+        return pltpu.make_async_copy(placed.at[k], out.at[k], leave_sem.at[k])
+
     for half in range(2):
-        for x in range(8):
-            if x % 4 == 0:
-                load(2 * half + x // 4).wait()
-            chunks = [landed[q, 8 * half + x] for q in range(4)]
-            for fl in range(4):
-                moved = [
-                    chunks[q] if q == fl else pltpu.roll(chunks[q], ((q - fl) * 32) % 128, 1)
-                    for q in range(4)
-                ]
-                low_half = jnp.where(lane < 32, moved[0], moved[1])
-                high_half = jnp.where(lane < 96, moved[2], moved[3])
-                flat[half, pl.ds(fl * 8 + x, 16, stride=32), :] = jnp.where(
-                    lane < 64, low_half, high_half
-                )
-        leave(half).start()
+        load(half).start()
     for half in range(2):
-        leave(half).wait()
+        load(half).wait()
+    for k in range(4):
+        for pair in range(8):
+            low, high = [
+                landed[half, pl.ds(8 * k + pair, 16, stride=32), :] for half in range(2)
+            ]
+            placed[k, 2 * pair] = jnp.where(lane < 64, low, pltpu.roll(high, 64, 1))
+            placed[k, 2 * pair + 1] = jnp.where(lane < 64, pltpu.roll(low, 64, 1), high)
+        leave(k).start()
+    for k in range(4):
+        leave(k).wait()
 
 
 def per_device(background_fields, obs_col, measured_height, obs_radius, obs_value, obs_var):
     dma = pltpu.SemaphoreType.DMA
     result = pl.pallas_call(
         kernel,
-        out_shape=jax.ShapeDtypeStruct((CHUNKS, 16, 16, 128), F32),
+        out_shape=jax.ShapeDtypeStruct((2, 512, 128), F32),
         in_specs=[pl.BlockSpec(memory_space=pltpu.HBM)] * 6,
         out_specs=pl.BlockSpec(memory_space=pltpu.HBM),
         scratch_shapes=[
@@ -574,8 +574,8 @@
             pltpu.VMEM((2, 8, 128), F32),
             pltpu.VMEM((2, 128), F32),
             pltpu.VMEM((3, 16, 2, 128), F32),
-            pltpu.VMEM((4, 128, 64), F32),
-            pltpu.VMEM((CHUNKS, 256, 128), F32),
+            pltpu.VMEM((8, 128, 64), F32),
+            pltpu.VMEM((2, 512, 128), F32),
             dma((6,)),
             dma((4,)),
             dma((4,)),
@@ -583,11 +583,11 @@
             dma((2,)),
             dma((3, 16)),
             dma((3,)),
-            dma((16,)),
-            dma((16,)),
-            dma((CHUNKS, 16)),
-            dma((CHUNKS, 16)),
-            dma((CHUNKS,)),
+            dma((4,)),
+            dma((4,)),
+            dma((2,)),
+            dma((2,)),
+            dma((2,)),
         ],
         compiler_params=pltpu.CompilerParams(
             collective_id=0, has_side_effects=True, vmem_limit_bytes=64 * 1024 * 1024
@@ -611,10 +611,10 @@
         in_specs=[pl.BlockSpec(memory_space=pltpu.HBM)],
         out_specs=pl.BlockSpec(memory_space=pltpu.HBM),
         scratch_shapes=[
-            pltpu.VMEM((CHUNKS, 16, 16, 128), F32),
-            pltpu.VMEM((2, 4, 16, 8, 128), F32),
+            pltpu.VMEM((2, 512, 128), F32),
+            pltpu.VMEM((4, 16, 16, 128), F32),
+            dma((2,)),
             dma((4,)),
-            dma((2,)),
         ],
         compiler_params=pltpu.CompilerParams(vmem_limit_bytes=60 * 1024 * 1024),
     )(result)

time: 51.8 us -> 47.7 us (0.921)
  the two profiles are of different devices: /device:TPU:1 before, /device:TPU:2 now
where the time goes in v2:
time: 47.7 us; the launch traced here: 47.5 us
  Pallas kernels  47.5 us (100%)
    pallas_call x1, Pallas kernels, per_device(): pl.pallas_call(kernel, out_shape=jax.ShapeDtypeStruct((2, 512, 128), F32)...  45.4 us
    pallas_call x1, Pallas kernels, per_device(): pl.pallas_call(place, out_shape=jax.ShapeDtypeStruct((4, 16, 16, 128), F3...  2.12 us

profile of v2, /device:TPU:2, one launch (start us, length us, event | category | flops | bytes accessed | tf_op | source)
XLA Modules:
  0.0 47.5 jit_solution(5925987035829692156)
XLA Ops:
  0.0 45.4 %shard_map.64.back_in = f32[2,512,128]{2,1,0:T(8,128)} custom-call(f32[1024,128]{1,0:T(8,128)} %bitcast.6, s32[16,128]{1,0:T(8,128)} %bitcast.7, s32[16,128]{1,0:T(8,128)} %bitcast.8, s32[1,64]{1,0:T(1,128)} %bitcast.9, f32[1,64]{1,0:T(1,128)} %bitcast.10, f32[1,64]{1,0:T(1,128)} %bitcast.11), custom_call_target="tpu_custom_call" | custom-call | tf_op jit(solution)/shard_map/pallas_call | solution.py:553
  45.4 2.1 %shard_map.65 = f32[4,16,16,128]{3,2,1,0:T(8,128)} custom-call(f32[2,512,128]{2,1,0:T(8,128)} %shard_map.64.back_in), custom_call_target="tpu_custom_call" | custom-call | tf_op jit(solution)/shard_map/pallas_call | solution.py:608

commit v3 on v2

--- a/solution.py
+++ b/solution.py
@@ -9,7 +9,8 @@
 COURANT = 0.6
 DIFFUSE = 0.1
 NS_PAIRS = 8
-EARLY = 1
+EARLY = 2
+LATER_EARLY = 0
 F32 = jnp.float32
 BF16 = jnp.bfloat16
 MESH = pl.DeviceIdType.MESH
@@ -58,6 +59,7 @@
     var,
     state,
     mid,
+    low_fields,
     fore,
     gathered,
     turned,
@@ -67,7 +69,11 @@
     side,
     side_in,
     picked,
+    partial,
+    beyond,
+    edge,
     picked_in,
+    beyond_in,
     stage,
     back,
     load_sem,
@@ -77,6 +83,12 @@
     side_recv,
     pick_send,
     pick_recv,
+    beyond_send,
+    beyond_recv,
+    ready,
+    partner_ready,
+    group_in,
+    mate_in,
     fore_send,
     fore_recv,
     back_send,
@@ -104,27 +116,36 @@
     for i in range(6):
         load(i).start()
 
+    core = lax.rem(tile, 2)
+    later = lax.rem(tile // 2, 2) == 1
+    mate = jnp.where(core == 0, right, left)
+    across = jnp.where(core == 0, left, right)
+
+    def signal(sem, device):
+        pl.semaphore_signal(sem, inc=1, device_id=device, device_id_type=MESH)
+
+    def over_group(action, start=0):
+        def body(d, carry):
+            action(lax.rem(me + d, group))
+            return carry
+
+        lax.fori_loop(start, group, body, 0)
+
     barrier = pltpu.get_barrier_semaphore()
 
-    def over_three(action):
-        def body(d, carry):
-            peer = lax.rem(me + d, group)
-            action(0, d, {"member": peer, "gx": right})
-            action(2, d, {"member": peer, "gx": left})
-
-            @pl.when(d > 0)
-            def _():
-                action(1, d, {"member": peer})
-
-            return carry
-
-        lax.fori_loop(0, group, body, 0)
-
-    over_three(
-        lambda rel, d, device: pl.semaphore_signal(
-            barrier, inc=1, device_id=device, device_id_type=MESH
-        )
-    )
+    @pl.when(later)
+    def _():
+        signal(barrier, {"gx": mate})
+        pl.semaphore_wait(barrier, group + 1)
+        signal(partner_ready, {"gx": across})
+        over_group(lambda peer: signal(ready, {"member": peer, "gx": across}), 1)
+
+    @pl.when(jnp.logical_not(later))
+    def _():
+        over_group(lambda peer: signal(barrier, {"member": peer, "gx": across}))
+        over_group(lambda peer: signal(barrier, {"member": peer}), 1)
+        over_group(lambda peer: signal(barrier, {"member": peer, "gx": mate}))
+
     for i in range(6):
         load(i).wait()
 
@@ -139,11 +160,15 @@
     side[...] = jnp.concatenate(
         [
             jnp.concatenate([value[...], var[...]], axis=1),
-            jnp.zeros((7, 128), F32),
+            jnp.concatenate([height[...].astype(F32), jnp.zeros((1, 64), F32)], axis=1),
+            jnp.zeros((6, 128), F32),
         ],
         axis=0,
     )
-    pl.semaphore_wait(barrier, 3 * group - 1)
+
+    @pl.when(jnp.logical_not(later))
+    def _():
+        pl.semaphore_wait(barrier, 2 * group - 1)
 
     def halo(direction, part):
         which = pl.ds(0, 1) if part == 0 else pl.ds(1, 3)
@@ -168,12 +193,29 @@
             device_id_type=MESH,
         )
 
-    for direction in range(2):
-        halo(direction, 0).start()
-    for direction in range(2):
-        to_side(direction).start()
-    for direction in range(2):
-        halo(direction, 1).start()
+    def to_mate():
+        for direction in range(2):
+
+            @pl.when(core == direction)
+            def _():
+                halo(direction, 0).start()
+                to_side(direction).start()
+                halo(direction, 1).start()
+
+    def to_across():
+        for direction in range(2):
+
+            @pl.when(core != direction)
+            def _():
+                halo(direction, 0).start()
+                to_side(direction).start()
+                halo(direction, 1).start()
+
+    @pl.when(later)
+    def _():
+        to_across()
+
+    to_mate()
 
     def first_step(index, which):
         mid[index, which] = advance(
@@ -181,132 +223,283 @@
         )
 
     def second_step(x, which):
-        fore[x, which] = advance(mid[x, which], mid[x + 1, which], mid[x + 2, which])
-
-    whole = pl.ds(0, 4)
-
-    def inner_first(i, carry):
-        for j in range(7):
-            first_step(2 + 7 * i + j, whole)
-        return carry
-
-    def inner_second(i, carry):
-        for j in range(6):
-            second_step(2 + 6 * i + j, whole)
-        return carry
-
-    lax.fori_loop(0, 2, inner_first, 0)
-    lax.fori_loop(0, 2, inner_second, 0)
-
-    def send_fore(fh, peer):
+        return advance(mid[x, which], mid[x + 1, which], mid[x + 2, which])
+
+    def pack(x, fields):
+        is_left = lax.broadcasted_iota(jnp.int32, (16, 128), 1) < 64
+        for fh in range(2):
+            a, b = fields[fh], fields[fh + 2]
+            fore[x, fh] = jnp.where(is_left, pltpu.roll(a, 64, 1), b)
+            fore[x, 2 + fh] = jnp.where(is_left, a, pltpu.roll(b, 64, 1))
+
+
+    def inner_rows(part):
+        which = pl.ds(0, 1) if part == 0 else pl.ds(1, 3)
+
+        def inner_first(i, carry):
+            for j in range(7):
+                first_step(2 + 7 * i + j, which)
+            return carry
+
+        def inner_second(i, carry):
+            for j in range(6):
+                x = 2 + 6 * i + j
+                fields = second_step(x, which)
+                if part == 0:
+                    low_fields[x] = fields[0]
+                else:
+                    pack(x, [low_fields[x], fields[0], fields[1], fields[2]])
+            return carry
+
+        lax.fori_loop(0, 2, inner_first, 0)
+        lax.fori_loop(0, 2, inner_second, 0)
+
+    def send_fore(piece, peer):
         return pltpu.make_async_remote_copy(
-            src_ref=fore.at[peer, fh],
-            dst_ref=gathered.at[fh, pl.ds(pl.multiple_of(me * 16, 16), 16), :],
-            send_sem=fore_send.at[fh],
-            recv_sem=fore_recv.at[fh],
+            src_ref=fore.at[peer, piece],
+            dst_ref=gathered.at[piece, pl.ds(pl.multiple_of(me * 16, 16), 16), :],
+            send_sem=fore_send.at[piece],
+            recv_sem=fore_recv.at[piece],
             device_id={"member": peer},
             device_id_type=MESH,
         )
 
     def over_peers(action):
-        def body(d, carry):
-            action(lax.rem(me + d, group))
-            return carry
-
-        lax.fori_loop(1, group, body, 0)
-
-    def start_fore(groups, inner):
+        over_group(action, 1)
+
+    def start_fore(inner_pieces, outer_pieces):
         def body(peer):
             is_inner = (peer >= 2) & (peer < 14)
 
-            @pl.when(is_inner if inner else jnp.logical_not(is_inner))
+            @pl.when(is_inner)
             def _():
-                for fh in groups:
-                    send_fore(fh, peer).start()
+                for piece in inner_pieces:
+                    send_fore(piece, peer).start()
+
+            @pl.when(jnp.logical_not(is_inner))
+            def _():
+                for piece in outer_pieces:
+                    send_fore(piece, peer).start()
 
         over_peers(body)
 
-    early, late = range(EARLY), range(EARLY, 4)
-    if EARLY:
-        start_fore(early, True)
-
-    def outer_rows(part):
+    def edge_rows(part, direction):
         which = pl.ds(0, 1) if part == 0 else pl.ds(1, 3)
         count = 1 if part == 0 else 3
-        for direction in range(2):
-            halo(direction, part).wait_recv()
+        halo(direction, part).wait_recv()
         nothing = jnp.zeros((count, 16, 128), F32)
-
-        @pl.when(tile == 0)
+        outside = tile == (0, tiles - 1)[direction]
+        slots, firsts, seconds, beyond = (
+            ((0, 1), (0, 1), (0, 1), 0),
+            ((18, 19), (16, 17), (14, 15), 17),
+        )[direction]
+
+        @pl.when(outside)
         def _():
-            state[0, which] = nothing
-            state[1, which] = nothing
-
-        @pl.when(tile == tiles - 1)
+            for slot in slots:
+                state[slot, which] = nothing
+
+        for index in firsts:
+            first_step(index, which)
+
+        @pl.when(outside)
         def _():
-            state[18, which] = nothing
-            state[19, which] = nothing
-
-        for index in (0, 1, 16, 17):
-            first_step(index, which)
-
-        @pl.when(tile == 0)
-        def _():
-            mid[0, which] = nothing
-
-        @pl.when(tile == tiles - 1)
-        def _():
-            mid[17, which] = nothing
-
-        for x in (0, 1, 14, 15):
-            second_step(x, which)
-
-    outer_rows(0)
+            mid[beyond, which] = nothing
+
+        for x in seconds:
+            fields = second_step(x, which)
+            if part == 0:
+                low_fields[x] = fields[0]
+            else:
+                pack(x, [low_fields[x], fields[0], fields[1], fields[2]])
 
     def tile_row(ref, t):
         row = ref[pl.ds(t // 2, 1), :]
         return jnp.where(lax.rem(t, 2) == 0, row[:, :64], row[:, 64:])
 
+    def hot(column):
+        rows = lax.broadcasted_iota(jnp.int32, (128, 64), 0)
+        return (rows == lax.rem(column, 128)).astype(F32).astype(BF16)
+
+    def sample(rows, hot_y, along, levels):
+        observed = jnp.concatenate(rows, axis=0)
+        hi, lo = split2(observed)
+        low = (observed - hi.astype(F32) - lo.astype(F32)).astype(BF16)
+        along_y = (matmul(hi, hot_y) + matmul(lo, hot_y)) + matmul(low, hot_y)
+        total = jnp.zeros((16, 64), F32)
+        for i, x in enumerate(along[1]):
+            total = total + jnp.where(along[0] == x, along_y[16 * i : 16 * i + 16], 0.0)
+        level = lax.rem(lax.broadcasted_iota(jnp.int32, (16, 64), 0), 4)
+        total = jnp.where(level == levels, total, 0.0)
+        sums = [jnp.sum(total[4 * k : 4 * k + 4], axis=0, keepdims=True) for k in range(4)]
+        return jnp.concatenate(
+            [
+                jnp.concatenate([sums[0], sums[1]], axis=1),
+                jnp.concatenate([sums[2], sums[3]], axis=1),
+            ],
+            axis=0,
+        )
+
     own_col = tile_row(col, tile)
     own_x = own_col // 128 - tile * 16
-    own_y = lax.rem(own_col, 128)
-    hot_y = (lax.broadcasted_iota(jnp.int32, (128, 64), 0) == own_y).astype(F32).astype(BF16)
-    observed = fore[:, 0].reshape(256, 128)
-    hi, lo = split2(observed)
-    low = (observed - hi.astype(F32) - lo.astype(F32)).astype(BF16)
-    along_y = (matmul(hi, hot_y) + matmul(lo, hot_y)) + matmul(low, hot_y)
-    total = jnp.zeros((16, 64), F32)
-    for x in range(16):
-        total = total + jnp.where(own_x == x, along_y[16 * x : 16 * x + 16], 0.0)
-    level = lax.rem(lax.broadcasted_iota(jnp.int32, (16, 64), 0), 4)
-    total = jnp.where(level == height[...], total, 0.0)
-    sums = [jnp.sum(total[4 * k : 4 * k + 4], axis=0, keepdims=True) for k in range(4)]
-    picked[...] = jnp.concatenate(
-        [
-            jnp.concatenate([sums[0], sums[1]], axis=1),
-            jnp.concatenate([sums[2], sums[3]], axis=1),
-        ],
-        axis=0,
-    )
-
-    def send_picked(rel, d, device):
+    hot_own = hot(own_col)
+
+    def own_samples():
+        rows = [low_fields[x] for x in range(16)]
+        return sample(rows, hot_own, (own_x, range(16)), height[...])
+
+    def send_picked(buffer, rel, device):
         return pltpu.make_async_remote_copy(
-            src_ref=picked,
+            src_ref=buffer,
             dst_ref=picked_in.at[rel, me],
-            send_sem=pick_send.at[rel, d],
+            send_sem=pick_send.at[rel],
             recv_sem=pick_recv.at[rel],
             device_id=device,
             device_id_type=MESH,
         )
 
-    over_three(lambda rel, d, device: send_picked(rel, d, device).start())
+    def send_beyond(device):
+        return pltpu.make_async_remote_copy(
+            src_ref=beyond,
+            dst_ref=beyond_in.at[me],
+            send_sem=beyond_send,
+            recv_sem=beyond_recv,
+            device_id=device,
+            device_id_type=MESH,
+        )
+
+    def over_tile(rel, action):
+        def body(d, carry):
+            peer = lax.rem(me + d, group)
+            action({"member": peer} if rel == 1 else {"member": peer, "gx": (right, 0, left)[rel]})
+            return carry
+
+        lax.fori_loop(1 if rel == 1 else 0, group, body, 0)
+
+    inner_rows(0)
+
+    @pl.when(jnp.logical_not(later))
+    def _():
+        inner_rows(1)
+        start_fore(range(EARLY), ())
+        pl.semaphore_wait(partner_ready, 1)
+        to_across()
+        pl.semaphore_wait(ready, group - 1)
+        signal(group_in, {"gx": across})
+
+    none = jnp.zeros((16, 128), F32)
+
+    @pl.when(core == 0)
+    def _():
+        edge_rows(0, 1)
+        first, second = state[2, 0], state[3, 0]
+        outer, inner = advance(none, none, first), advance(none, first, second)
+        low_fields[0] = advance(outer, inner, mid[2, 0])
+        low_fields[1] = advance(inner, mid[2, 0], mid[3, 0])
+        edge[0] = advance(none, none, outer)
+        edge[1] = advance(none, outer, inner)
+
+    @pl.when(core == 1)
+    def _():
+        edge_rows(0, 0)
+        first, second = state[17, 0], state[16, 0]
+        outer, inner = advance(first, none, none), advance(second, first, none)
+        low_fields[15] = advance(mid[15, 0], inner, outer)
+        low_fields[14] = advance(mid[14, 0], mid[15, 0], inner)
+        edge[0] = advance(inner, outer, none)
+        edge[1] = advance(outer, none, none)
+
+    @pl.when(later)
+    def _():
+        partial[...] = own_samples()
+
+        @pl.when(core == 0)
+        def _():
+            over_tile(2, lambda device: send_picked(partial, 2, device).start())
+
+        @pl.when(core == 1)
+        def _():
+            over_tile(0, lambda device: send_picked(partial, 0, device).start())
+
+    @pl.when(later)
+    def _():
+        inner_rows(1)
+        pl.semaphore_wait(group_in, 1)
+        signal(mate_in, {"gx": mate})
+        start_fore(range(LATER_EARLY), ())
+        pl.semaphore_wait(mate_in, 1)
+
+    @pl.when(core == 0)
+    def _():
+        edge_rows(0, 0)
+
+    @pl.when(core == 1)
+    def _():
+        edge_rows(0, 1)
+
+    for direction in range(2):
+        to_side(direction).wait_recv()
+    picked[...] = own_samples()
+    over_tile(1, lambda device: send_picked(picked, 1, device).start())
+
+    @pl.when(core == 0)
+    def _():
+        over_tile(0, lambda device: send_picked(picked, 0, device).start())
+
+    @pl.when(core == 1)
+    def _():
+        over_tile(2, lambda device: send_picked(picked, 2, device).start())
+
+    @pl.when(jnp.logical_not(later))
+    def _():
+        across_col = tile_row(col, across)
+        across_x = across_col // 128 - across * 16 - jnp.where(core == 0, 14, 0)
+        levels = jnp.where(core == 0, side_in[0, 1:2, :64], side_in[1, 1:2, :64])
+        beyond[...] = sample(
+            [edge[0], edge[1]],
+            hot(across_col),
+            (across_x, range(2)),
+            levels.astype(jnp.int32),
+        )
+        beyond_in[me] = beyond[...]
+        over_tile(1, lambda device: send_beyond(device).start())
+
+        @pl.when(core == 0)
+        def _():
+            over_tile(2, lambda device: send_picked(picked, 2, device).start())
+
+        @pl.when(core == 1)
+        def _():
+            over_tile(0, lambda device: send_picked(picked, 0, device).start())
+
+    @pl.when(later)
+    def _():
+        beyond_in[...] = jnp.zeros((16, 2, 128), F32)
+
     picked_in[1, me] = picked[...]
-    if EARLY:
-        start_fore(range(1), False)
-    start_fore(late, True)
-
-    outer_rows(1)
-    start_fore(range(min(EARLY, 1), 4), False)
+
+    @pl.when(later)
+    def _():
+        start_fore(range(LATER_EARLY, 2), ())
+
+    if EARLY < 2:
+
+        @pl.when(jnp.logical_not(later))
+        def _():
+            start_fore(range(EARLY, 2), ())
+
+    for direction in range(2):
+        edge_rows(1, direction)
+    start_fore((), range(2))
+
+    @pl.when(later)
+    def _():
+        start_fore(range(2, 4), range(2, 4))
+
+    @pl.when(jnp.logical_not(later))
+    def _():
+        start_fore(range(max(EARLY, 2), 4), range(2, 4))
+
     gathered[:, pl.ds(pl.multiple_of(me * 16, 16), 16), :] = fore[me]
 
     def three(a, b, c, fill):
@@ -318,8 +511,6 @@
     near_radius = three(
         tile_row(radius, before), tile_row(radius, tile), tile_row(radius, after), 1
     ).astype(F32)
-    for direction in range(2):
-        to_side(direction).wait_recv()
     from_left, own, from_right = side_in[0, 0:1, :], side[0:1, :], side_in[1, 0:1, :]
     near_value = three(from_left[:, :64], own[:, :64], from_right[:, :64], 0.0)
     near_var = three(from_left[:, 64:], own[:, 64:], from_right[:, 64:], 1.0)
@@ -337,22 +528,30 @@
     )
     wgt[...] = taper * inverse
 
-    def arrived(rel):
-        count = 15 if rel == 1 else 16
-        pltpu.make_async_copy(
-            picked_in.at[rel, pl.ds(0, count)],
-            picked_in.at[rel, pl.ds(0, count)],
-            pick_recv.at[rel],
-        ).wait()
-
-    def by_member(rel):
-        rows = jnp.concatenate([picked_in[rel, m] for m in range(16)], axis=0)
+    def arrived(buffer, count, sem):
+        rows = buffer.at[pl.ds(0, count)]
+        pltpu.make_async_copy(rows, rows, sem).wait()
+
+    def by_member(buffer):
+        rows = jnp.concatenate([buffer[m] for m in range(16)], axis=0)
         return jnp.concatenate([rows[:, :64], rows[:, 64:]], axis=0)
 
     for rel in range(3):
-        arrived(rel)
+        arrived(picked_in.at[rel], 15 if rel == 1 else 16, pick_recv.at[rel])
+
+    @pl.when(jnp.logical_not(later))
+    def _():
+        arrived(beyond_in, 15, beyond_recv)
+
+    added = by_member(beyond_in)
     ensemble = jnp.concatenate(
-        [by_member(rel) for rel in range(3)] + [jnp.zeros((64, 64), F32)], axis=1
+        [
+            by_member(picked_in.at[0]) + jnp.where(core == 0, added, 0.0),
+            by_member(picked_in.at[1]),
+            by_member(picked_in.at[2]) + jnp.where(core == 1, added, 0.0),
+            jnp.zeros((64, 64), F32),
+        ],
+        axis=1,
     )
     mean = jnp.sum(ensemble, axis=0, keepdims=True) / 64.0
     spread = ensemble - mean
@@ -461,16 +660,20 @@
             back.at[half, rows], back_in.at[half, rows], keep_sem.at[half]
         )
 
-    def turn(fh):
+    def turn(half, fh):
+        piece = 2 * (1 - half) + fh
+        all_bytes(gathered.at[piece], fore_recv.at[piece]).wait()
         for fl in range(4):
             rows = jnp.concatenate(
-                [gathered[fh, pl.ds(fl + 4 * odd, 32, stride=8), :] for odd in range(2)], axis=0
+                [gathered[piece, pl.ds(fl + 4 * odd, 32, stride=8), :] for odd in range(2)], axis=0
             )
-            turned[fh * 4 + fl] = jnp.concatenate([rows, rows], axis=0).T
+            columns = jnp.concatenate([rows, rows], axis=0).T
+            turned[4 * fh + fl] = columns[:64]
+            turned[8 + 4 * fh + fl] = columns[64:]
 
     def blend(half, part):
         block = half * 8 + part
-        rows = turned[:, pl.ds(pl.multiple_of(block * 8, 8), 8), :]
+        rows = turned[:, 8 * part : 8 * part + 8, :]
         near = operand((rows * coef_a).reshape(128, 128))
         far = operand((rows * coef_b).reshape(128, 128))
         c01 = weights[pl.ds(2 * block, 2)].reshape(128, 128)
@@ -490,10 +693,9 @@
         def _():
             weights[32] = weights[31]
             weights[33] = jnp.zeros((64, 128), BF16)
-            for fh in range(4):
-                all_bytes(gathered.at[fh], fore_recv.at[fh]).wait()
-                turn(fh)
-
+
+        for fh in range(2):
+            turn(half, fh)
         for part in range(8):
             blend(half, part)
         for pair in range(8):
@@ -513,7 +715,13 @@
             halo(direction, part).wait_send()
     for direction in range(2):
         to_side(direction).wait_send()
-    over_three(lambda rel, d, device: send_picked(rel, d, device).wait_send())
+    for rel in range(3):
+        arrived(picked_in.at[rel], 15 if rel == 1 else 16, pick_send.at[rel])
+
+    @pl.when(jnp.logical_not(later))
+    def _():
+        arrived(beyond_in, 15, beyond_send)
+
     for fh in range(4):
         all_bytes(gathered.at[fh], fore_send.at[fh]).wait()
     for half in range(2):
@@ -564,16 +772,21 @@
             pltpu.VMEM((1, 64), F32),
             pltpu.VMEM((20, 4, 16, 128), F32),
             pltpu.VMEM((18, 4, 16, 128), F32),
+            pltpu.VMEM((16, 16, 128), F32),
             pltpu.VMEM((16, 4, 16, 128), F32),
             pltpu.VMEM((4, 256, 128), F32),
-            pltpu.VMEM((16, 128, 128), F32),
+            pltpu.VMEM((16, 64, 128), F32),
             pltpu.VMEM((34, 64, 128), BF16),
             pltpu.VMEM((32, 256), F32),
             pltpu.VMEM((64, 256), F32),
             pltpu.VMEM((8, 128), F32),
             pltpu.VMEM((2, 8, 128), F32),
             pltpu.VMEM((2, 128), F32),
+            pltpu.VMEM((2, 128), F32),
+            pltpu.VMEM((2, 128), F32),
+            pltpu.VMEM((2, 16, 128), F32),
             pltpu.VMEM((3, 16, 2, 128), F32),
+            pltpu.VMEM((16, 2, 128), F32),
             pltpu.VMEM((8, 128, 64), F32),
             pltpu.VMEM((2, 512, 128), F32),
             dma((6,)),
@@ -581,8 +794,14 @@
             dma((4,)),
             dma((2,)),
             dma((2,)),
-            dma((3, 16)),
             dma((3,)),
+            dma((3,)),
+            dma,
+            dma,
+            pltpu.SemaphoreType.REGULAR,
+            pltpu.SemaphoreType.REGULAR,
+            pltpu.SemaphoreType.REGULAR,
+            pltpu.SemaphoreType.REGULAR,
             dma((4,)),
             dma((4,)),
             dma((2,)),

time: 47.7 us -> 44.3 us (0.929)
  the two profiles are of different devices: /device:TPU:2 before, /device:TPU:24 now
where the time goes in v3:
time: 44.3 us; the launch traced here: 44.2 us
  Pallas kernels  44.1 us (100%)
    pallas_call x1, Pallas kernels, per_device(): pl.pallas_call(kernel, out_shape=jax.ShapeDtypeStruct((2, 512, 128), F32)...  42 us
    pallas_call x1, Pallas kernels, per_device(): pl.pallas_call(place, out_shape=jax.ShapeDtypeStruct((4, 16, 16, 128), F3...  2.12 us

profile of v3, /device:TPU:24, one launch (start us, length us, event | category | flops | bytes accessed | tf_op | source)
XLA Modules:
  0.0 44.2 jit_solution(508787876687193294)
XLA Ops:
  0.0 42.0 %shard_map.64.back_in = f32[2,512,128]{2,1,0:T(8,128)} custom-call(f32[1024,128]{1,0:T(8,128)} %bitcast.6, s32[16,128]{1,0:T(8,128)} %bitcast.7, s32[16,128]{1,0:T(8,128)} %bitcast.8, s32[1,64]{1,0:T(1,128)} %bitcast.9, f32[1,64]{1,0:T(1,128)} %bitcast.10, f32[1,64]{1,0:T(1,128)} %bitcast.11), custom_call_target="tpu_custom_call" | custom-call | tf_op jit(solution)/shard_map/pallas_call | solution.py:761
  42.0 2.1 %shard_map.65 = f32[4,16,16,128]{3,2,1,0:T(8,128)} custom-call(f32[2,512,128]{2,1,0:T(8,128)} %shard_map.64.back_in), custom_call_target="tpu_custom_call" | custom-call | tf_op jit(solution)/shard_map/pallas_call | solution.py:827

commit v4 on v3

--- a/solution.py
+++ b/solution.py
@@ -10,7 +10,7 @@
 DIFFUSE = 0.1
 NS_PAIRS = 8
 EARLY = 2
-LATER_EARLY = 0
+LATER_EARLY = 1
 F32 = jnp.float32
 BF16 = jnp.bfloat16
 MESH = pl.DeviceIdType.MESH
@@ -384,8 +384,6 @@
         start_fore(range(EARLY), ())
         pl.semaphore_wait(partner_ready, 1)
         to_across()
-        pl.semaphore_wait(ready, group - 1)
-        signal(group_in, {"gx": across})
 
     none = jnp.zeros((16, 128), F32)
 
@@ -428,6 +426,11 @@
         signal(mate_in, {"gx": mate})
         start_fore(range(LATER_EARLY), ())
         pl.semaphore_wait(mate_in, 1)
+
+    @pl.when(jnp.logical_not(later))
+    def _():
+        pl.semaphore_wait(ready, group - 1)
+        signal(group_in, {"gx": across})
 
     @pl.when(core == 0)
     def _():
@@ -733,22 +736,20 @@
 
 def place(back_in, out, landed, placed, load_sem, leave_sem):
     lane = lax.broadcasted_iota(jnp.int32, (16, 128), 1)
-
-    def load(half):
-        return pltpu.make_async_copy(back_in.at[half], landed.at[half], load_sem.at[half])
+    flat = landed.reshape(4, 2, 128, 128)
+
+    def load(k):
+        return pltpu.make_async_copy(back_in.at[:, :, k], landed.at[k], load_sem.at[k])
 
     def leave(k):
         return pltpu.make_async_copy(placed.at[k], out.at[k], leave_sem.at[k])
 
-    for half in range(2):
-        load(half).start()
-    for half in range(2):
-        load(half).wait()
     for k in range(4):
+        load(k).start()
+    for k in range(4):
+        load(k).wait()
         for pair in range(8):
-            low, high = [
-                landed[half, pl.ds(8 * k + pair, 16, stride=32), :] for half in range(2)
-            ]
+            low, high = [flat[k, half, pl.ds(pair, 16, stride=8), :] for half in range(2)]
             placed[k, 2 * pair] = jnp.where(lane < 64, low, pltpu.roll(high, 64, 1))
             placed[k, 2 * pair + 1] = jnp.where(lane < 64, pltpu.roll(low, 64, 1), high)
         leave(k).start()
@@ -830,13 +831,13 @@
         in_specs=[pl.BlockSpec(memory_space=pltpu.HBM)],
         out_specs=pl.BlockSpec(memory_space=pltpu.HBM),
         scratch_shapes=[
-            pltpu.VMEM((2, 512, 128), F32),
+            pltpu.VMEM((4, 2, 16, 8, 128), F32),
             pltpu.VMEM((4, 16, 16, 128), F32),
-            dma((2,)),
+            dma((4,)),
             dma((4,)),
         ],
         compiler_params=pltpu.CompilerParams(vmem_limit_bytes=60 * 1024 * 1024),
-    )(result)
+    )(result.reshape(2, 16, 4, 8, 128))
 
 
 def solution(mesh):

time: 44.3 us -> 44.2 us (level)
  no operation moved by 1% of the time
where the time goes in v4:
time: 44.2 us; the launch traced here: 44.1 us
  Pallas kernels  44.1 us (100%)
    pallas_call x1, Pallas kernels, per_device(): pl.pallas_call(kernel, out_shape=jax.ShapeDtypeStruct((2, 512, 128), F32)...  42 us
    pallas_call x1, Pallas kernels, per_device(): pl.pallas_call(place, out_shape=jax.ShapeDtypeStruct((4, 16, 16, 128), F3...  2.05 us

profile of v4, /device:TPU:24, one launch (start us, length us, event | category | flops | bytes accessed | tf_op | source)
XLA Modules:
  0.0 44.1 jit_solution(14127366186996875146)
XLA Ops:
  0.0 42.0 %shard_map.64 = f32[2,512,128]{2,1,0:T(8,128)} custom-call(f32[1024,128]{1,0:T(8,128)} %bitcast.8, s32[16,128]{1,0:T(8,128)} %bitcast.9, s32[16,128]{1,0:T(8,128)} %bitcast.10, s32[1,64]{1,0:T(1,128)} %bitcast.11, f32[1,64]{1,0:T(1,128)} %bitcast.12, f32[1,64]{1,0:T(1,128)} %bitcast.13), custom_call_target="tpu_custom_call" | custom-call | tf_op jit(solution)/shard_map/pallas_call | solution.py:762
  42.0 2.0 %shard_map.65 = f32[4,16,16,128]{3,2,1,0:T(8,128)} custom-call(f32[2,16,4,8,128]{4,3,2,1,0:T(8,128)} %bitcast.7), custom_call_target="tpu_custom_call" | custom-call | tf_op jit(solution)/shard_map/pallas_call | solution.py:828

commit v5 on v4

--- a/solution.py
+++ b/solution.py
@@ -136,9 +136,6 @@
     @pl.when(later)
     def _():
         signal(barrier, {"gx": mate})
-        pl.semaphore_wait(barrier, group + 1)
-        signal(partner_ready, {"gx": across})
-        over_group(lambda peer: signal(ready, {"member": peer, "gx": across}), 1)
 
     @pl.when(jnp.logical_not(later))
     def _():
@@ -169,6 +166,11 @@
     @pl.when(jnp.logical_not(later))
     def _():
         pl.semaphore_wait(barrier, 2 * group - 1)
+
+    @pl.when(later)
+    def _():
+        pl.semaphore_wait(barrier, group + 1)
+        signal(partner_ready, {"gx": across})
 
     def halo(direction, part):
         which = pl.ds(0, 1) if part == 0 else pl.ds(1, 3)
@@ -214,6 +216,7 @@
     @pl.when(later)
     def _():
         to_across()
+        over_group(lambda peer: signal(ready, {"member": peer, "gx": across}), 1)
 
     to_mate()
 

time: 44.2 us -> 44.1 us (level)
  no operation moved by 1% of the time
where the time goes in v5:
time: 44.1 us; the launch traced here: 44 us
  Pallas kernels  44 us (100%)
    pallas_call x1, Pallas kernels, per_device(): pl.pallas_call(kernel, out_shape=jax.ShapeDtypeStruct((2, 512, 128), F32)...  41.9 us
    pallas_call x1, Pallas kernels, per_device(): pl.pallas_call(place, out_shape=jax.ShapeDtypeStruct((4, 16, 16, 128), F3...  2.05 us

profile of v5, /device:TPU:24, one launch (start us, length us, event | category | flops | bytes accessed | tf_op | source)
XLA Modules:
  0.0 44.0 jit_solution(8241988414454252641)
XLA Ops:
  0.0 41.9 %shard_map.64 = f32[2,512,128]{2,1,0:T(8,128)} custom-call(f32[1024,128]{1,0:T(8,128)} %bitcast.8, s32[16,128]{1,0:T(8,128)} %bitcast.9, s32[16,128]{1,0:T(8,128)} %bitcast.10, s32[1,64]{1,0:T(1,128)} %bitcast.11, f32[1,64]{1,0:T(1,128)} %bitcast.12, f32[1,64]{1,0:T(1,128)} %bitcast.13), custom_call_target="tpu_custom_call" | custom-call | tf_op jit(solution)/shard_map/pallas_call | solution.py:765
  41.9 2.0 %shard_map.65 = f32[4,16,16,128]{3,2,1,0:T(8,128)} custom-call(f32[2,16,4,8,128]{4,3,2,1,0:T(8,128)} %bitcast.7), custom_call_target="tpu_custom_call" | custom-call | tf_op jit(solution)/shard_map/pallas_call | solution.py:831

commit v6 on v4

--- a/solution.py
+++ b/solution.py
@@ -690,6 +690,8 @@
 
     def half_step(step, carry):
         half = 1 - step
+        for fh in range(2):
+            turn(half, fh)
         solve(half)
 
         @pl.when(step == 0)
@@ -697,8 +699,6 @@
             weights[32] = weights[31]
             weights[33] = jnp.zeros((64, 128), BF16)
 
-        for fh in range(2):
-            turn(half, fh)
         for part in range(8):
             blend(half, part)
         for pair in range(8):

time: 44.2 us -> 43.9 us (level)
  no operation moved by 1% of the time
where the time goes in v6:
time: 43.9 us; the launch traced here: 43.7 us
  Pallas kernels  43.7 us (100%)
    pallas_call x1, Pallas kernels, per_device(): pl.pallas_call(kernel, out_shape=jax.ShapeDtypeStruct((2, 512, 128), F32)...  41.7 us
    pallas_call x1, Pallas kernels, per_device(): pl.pallas_call(place, out_shape=jax.ShapeDtypeStruct((4, 16, 16, 128), F3...  2.05 us

profile of v6, /device:TPU:24, one launch (start us, length us, event | category | flops | bytes accessed | tf_op | source)
XLA Modules:
  0.0 43.7 jit_solution(17362679447781840079)
XLA Ops:
  0.0 41.7 %shard_map.64 = f32[2,512,128]{2,1,0:T(8,128)} custom-call(f32[1024,128]{1,0:T(8,128)} %bitcast.8, s32[16,128]{1,0:T(8,128)} %bitcast.9, s32[16,128]{1,0:T(8,128)} %bitcast.10, s32[1,64]{1,0:T(1,128)} %bitcast.11, f32[1,64]{1,0:T(1,128)} %bitcast.12, f32[1,64]{1,0:T(1,128)} %bitcast.13), custom_call_target="tpu_custom_call" | custom-call | tf_op jit(solution)/shard_map/pallas_call | solution.py:762
  41.7 2.0 %shard_map.65 = f32[4,16,16,128]{3,2,1,0:T(8,128)} custom-call(f32[2,16,4,8,128]{4,3,2,1,0:T(8,128)} %bitcast.7), custom_call_target="tpu_custom_call" | custom-call | tf_op jit(solution)/shard_map/pallas_call | solution.py:828
